TPU v7x, 256 devices: a whole 4x4x8 slice. The times are simulated.
256 devices in a mesh: band: 16 (over z_lo, y), plane: 16 (over x, z_hi, core).
Axes of the slice: x: 4, y: 4, z: 8 (z_hi: 2, z_lo: 4; z = z_hi * 4 + z_lo), core: 2. Of those that a mesh axis runs over, the one named last changes fastest.
Arguments:
- coeffs: float32 [16, 4, 65, 2048], P('band', None, None, 'plane'), may hold values from -6 to 6
- potential: float32 [128, 128, 128], P('plane', 'band'), may hold values from -6 to 6
- stick_map: int32 [3, 2048], replicated, may hold values from -32 to 32, as said below
Outputs:
- applied_coeffs: float32 [16, 4, 65, 2048], P('band', None, None, 'plane')
Inputs may be any that keep to these rules, and one draw needn't show every extreme that they name: `stick_map`: column s describes stick slot s: rows 0 and 1 are its G_x and G_y, row 2 its half-height h, or -1 for an empty slot (then G_x = G_y = 0). The live slots hold every column (x, y) with x*x + y*y <= 32 squared and x > 0, or x = 0 and y > 0, exactly once, with h the largest integer for which x*x + y*y + h*h <= 32 squared. Which slot holds which column is drawn.
All inputs are finite; a program needn't handle non-finite values.
Results may differ from a plain program's by a relative error of at most 0.00007.
Values sent between devices are 32-bit elements; how exact they have to be, the bound alone decides.
A program may use at most 64 MiB of HBM per device.

v0:
```python
import functools

import jax
import jax.numpy as jnp
import ml_dtypes
import numpy as np
from jax import lax
from jax.experimental import pallas as pl
from jax.experimental.pallas import tpu as pltpu
from jax.sharding import PartitionSpec as P

MESH = pl.DeviceIdType.MESH
GRID = 128
RADIUS = 32
BF = jnp.bfloat16
F32 = jnp.float32


def _halves(table):
    high = table.astype(ml_dtypes.bfloat16)
    low = (table - high.astype(np.float64)).astype(ml_dtypes.bfloat16)
    return high, low


def _left(table):
    high, low = _halves(table)
    return np.concatenate([high, low, high], axis=1)


def _right(table):
    high, low = _halves(table)
    return np.concatenate([high, low, high], axis=0)


def _trig(left, right):
    turns = np.mod(np.outer(left, right), GRID) * (2.0 * np.pi / GRID)
    return np.cos(turns), np.sin(turns)


def tables():
    points = np.arange(GRID)
    depth = np.arange(2 * RADIUS + 1) - RADIUS
    span = depth.size
    cos, sin = _trig(points, depth)
    zf = np.zeros((16, 2, 8, 2, 80))
    cos, sin = cos.reshape(16, 8, span), sin.reshape(16, 8, span)
    zf[:, 0, :, 0, :span], zf[:, 0, :, 1, :span] = cos, -sin
    zf[:, 1, :, 0, :span], zf[:, 1, :, 1, :span] = sin, cos
    zf = _left(zf.reshape(256, 160))
    zb = np.zeros((2, 72, 16, 2, 8))
    cos, sin = np.moveaxis(cos, 2, 0), np.moveaxis(sin, 2, 0)
    zb[0, :span, :, 0], zb[0, :span, :, 1] = cos, sin
    zb[1, :span, :, 0], zb[1, :span, :, 1] = -sin, cos
    zb = _left(zb.reshape(144, 256))
    cos, sin = _trig(np.arange(64) - 31, points)
    wy = np.zeros((2, 2, 64, 2, GRID))
    wb = np.zeros((2, 2, GRID, 2, 2, 64))
    for i in range(2):
        wy[i, i, :, 0], wy[i, i, :, 1] = cos, sin
        wb[i, 0, :, 0, i], wb[i, 1, :, 0, i] = cos.T, sin.T
        wb[i, 0, :, 1, i], wb[i, 1, :, 1, i] = -sin.T, cos.T
    wy = np.stack([_right(wy[i].reshape(128, 256)) for i in range(2)])
    wb = _right(wb.reshape(512, 256))
    cos, sin = _trig(np.arange(32), points)
    base = np.zeros((5, 2, 8, GRID))
    base[:4, 0], base[:4, 1] = cos.reshape(4, 8, GRID), -sin.reshape(4, 8, GRID)
    cos, sin = _trig(np.array([RADIUS]), points)
    base[4, 0, 0], base[4, 1, 0] = cos[0] - 1.0, -sin[0]
    base = base.reshape(80, GRID)
    xf, xb = _left(base.T), _left(base)
    return zf, wy, xf, xb, wb, zb


def halves(value):
    high = value.astype(BF)
    return high, (value - high.astype(F32)).astype(BF)


def mm(left, right):
    return jnp.dot(left, right, preferred_element_type=F32)


def kernel(
    n_z, n_y,
    c_ref, p_ref, sm_ref, zf_h, wy_h, xf_h, xb_h, wb_h, zb_h,
    o_ref,
    zf, wy, xf, xb, wb, zb,
    xs, zs, r1, s2, r2, slab, lt, dm, m1, gs, bs, cs, sp, og,
    c_sem, a_s, a_r, b_s, b_r, gz_s, gz_r, gy_s, gy_r, own_sem,
):
    band = lax.axis_index("band")
    me = lax.axis_index("plane")
    z_me, y_me = band // n_y, lax.rem(band, n_y)
    span = c_ref.shape[2]

    loads = [
        pltpu.make_async_copy(src, dst, c_sem.at[n])
        for n, (src, dst) in enumerate(
            [(zf_h, zf), (wy_h, wy), (xf_h, xf), (xb_h, xb), (wb_h, wb), (zb_h, zb)]
        )
    ]
    for load in loads:
        load.start()

    def z_peer(k):
        return lax.rem(z_me + k, n_z) * n_y + y_me

    def y_peer(k):
        return z_me * n_y + lax.rem(y_me + k, n_y)

    barrier = pltpu.get_barrier_semaphore()
    for k in range(1, 16):
        pl.semaphore_signal(
            barrier, inc=1, device_id={"plane": lax.rem(me + k, 16)}, device_id_type=MESH
        )
    for k in range(1, n_z):
        pl.semaphore_signal(barrier, inc=1, device_id={"band": z_peer(k)}, device_id_type=MESH)
    for k in range(1, n_y):
        pl.semaphore_signal(barrier, inc=1, device_id={"band": y_peer(k)}, device_id_type=MESH)

    heights = sm_ref[2:3, pl.ds(pl.multiple_of(me * 128, 128), 128)]
    live = jnp.abs(lax.broadcasted_iota(jnp.int32, (span, 128), 0) - RADIUS) <= heights
    xs[:, 64:80, :] = jnp.zeros((2, 16, 256), F32)
    for orb in range(2):
        for c in range(2):
            xs[c, 0:span, orb * 128 : orb * 128 + 128] = jnp.where(
                live, c_ref[0, 2 * orb + c], 0.0
            )
    high, low = halves(xs[...].reshape(160, 256))
    loads[0].wait()
    zs[...] = mm(zf[...], jnp.concatenate([high, high, low], axis=0)).reshape(16, 16, 256)

    pl.semaphore_wait(barrier, 15 + n_z - 1 + n_y - 1)

    def a_copy(k):
        to = lax.rem(me + k, 16)
        return pltpu.make_async_remote_copy(
            src_ref=zs.at[to], dst_ref=r1.at[me],
            send_sem=a_s.at[k], recv_sem=a_r.at[k],
            device_id={"plane": to}, device_id_type=MESH,
        )

    def b_copy(k):
        to = lax.rem(me + k, 16)
        return pltpu.make_async_remote_copy(
            src_ref=s2.at[to], dst_ref=r2.at[me],
            send_sem=b_s.at[k], recv_sem=b_r.at[k],
            device_id={"plane": to}, device_id_type=MESH,
        )

    def gz_copy(k):
        return pltpu.make_async_remote_copy(
            src_ref=p_ref, dst_ref=slab.at[y_me, z_me],
            send_sem=gz_s.at[k], recv_sem=gz_r.at[k],
            device_id={"band": z_peer(k)}, device_id_type=MESH,
        )

    def gy_copy(k):
        return pltpu.make_async_remote_copy(
            src_ref=slab.at[y_me], dst_ref=slab.at[y_me],
            send_sem=gy_s.at[k], recv_sem=gy_r.at[k],
            device_id={"band": y_peer(k)}, device_id_type=MESH,
        )

    for k in range(1, n_z):
        gz_copy(k).start()
    for k in range(1, 16):
        a_copy(k).start()
    own = pltpu.make_async_copy(p_ref, slab.at[y_me, z_me], own_sem)
    own.start()
    r1[me] = zs[me]

    stick_x, stick_y = sm_ref[0:1, :], sm_ref[1:2, :]
    d_of = stick_x & 7
    lane_of = ((stick_x >> 3) & 3) * 64 + stick_y + 31
    for n in range(16):
        rows = lax.broadcasted_iota(jnp.int32, (16, 2048), 0) + n * 16
        lt[n * 16 : n * 16 + 16, :] = jnp.where(rows == lane_of, 1.0, 0.0).astype(BF)
    d_rows = jnp.broadcast_to(d_of, (16, 2048))
    for d in range(8):
        dm[d] = jnp.where(d_rows == d, 1.0, 0.0).astype(BF)

    own.wait()
    for k in range(1, n_z):
        gz_copy(k).wait_recv()
    for k in range(1, n_y):
        gy_copy(k).start()

    for k in range(1, 16):
        a_copy(k).wait_recv()

    for r in range(16):
        lanes = slice(r * 128, r * 128 + 128)
        for h, part in enumerate(halves(r1[r])):
            for orb in range(2):
                piece = part[:, orb * 128 : orb * 128 + 128]
                for d in range(8):
                    at = h * 256 + orb * 128 + d * 16
                    m1[at : at + 16, lanes] = piece * dm[d, :, lanes]
    both = lax.dot_general(
        m1[...], lt[...], (((1,), (1,)), ((), ())), preferred_element_type=F32
    )
    both = both[:256] + both[256:]
    for hx in range(2):
        gs[hx] = both[:, hx * 128 : hx * 128 + 128]
    grid = [
        jnp.concatenate(
            [
                gs[hx, pl.ds(orb * 128 + c * 8 + z, 8, stride=16), :]
                for orb in range(2)
                for z in range(8)
                for c in range(2)
            ],
            axis=0,
        )
        for hx in range(2)
    ]

    def keep(value, at):
        high, low = halves(value)
        for orb in range(2):
            lanes = slice(orb * 128, orb * 128 + 128)
            bs[:, at : at + 16, lanes] = high[orb]
            bs[:, 80 + at : 96 + at, lanes] = high[orb]
            bs[:, 160 + at : 176 + at, lanes] = low[orb]

    loads[1].wait()
    for hx in range(2):
        high, low = halves(grid[hx])
        left = jnp.concatenate([high, high, low], axis=1)
        for i in range(2):
            turned = mm(left, wy[i]).reshape(2, 8, 2, 8, 256)
            real = turned[:, :, 0, :, :128] - turned[:, :, 1, :, 128:]
            imag = turned[:, :, 0, :, 128:] + turned[:, :, 1, :, :128]
            keep(jnp.concatenate([real, imag], axis=2), (2 * hx + i) * 16)
    keep(jnp.broadcast_to(grid[0][:, 31:32], (256, 128)).reshape(2, 8, 16, 128), 64)

    for k in range(1, n_y):
        gy_copy(k).wait_recv()
    loads[2].wait()
    loads[3].wait()

    for z in range(8):
        field = mm(xf[...], bs[z])
        plane = jnp.concatenate(
            [slab[b % n_y, b // n_y, z] for b in range(n_z * n_y)], axis=0
        )
        high, low = halves(field * jnp.concatenate([plane, plane], axis=1))
        back = mm(xb[...], jnp.concatenate([high, high, low], axis=0))
        for orb in range(2):
            lanes = slice(orb * 128, orb * 128 + 128)
            rows = slice(orb * 64 + z * 8, orb * 64 + z * 8 + 8)
            for xl in range(4):
                for c in range(2):
                    at = ((xl % 2) * 2 + c) * 128
                    cs[xl // 2, rows, at : at + 128] = back[
                        (xl * 2 + c) * 8 : (xl * 2 + c) * 8 + 8, lanes
                    ]
            for c in range(2):
                sp[c, rows, :] = back[64 + c * 8 : 72 + c * 8, lanes]

    loads[4].wait()
    at_zero = lax.broadcasted_iota(jnp.int32, (128, 128), 1) == 31
    for hx in range(2):
        high, low = halves(cs[hx])
        turned = mm(jnp.concatenate([high, high, low], axis=1), wb[...])
        for c in range(2):
            part = turned[:, c * 128 : c * 128 + 128]
            if hx == 0:
                part = part + jnp.where(at_zero, jnp.sum(sp[c], axis=1, keepdims=True), 0.0)
            og[hx, c * 128 : c * 128 + 128, :] = part

    picked = jnp.concatenate(
        [
            jnp.concatenate(
                [og[hx, pl.ds(c * 128 + d, 16, stride=8), :] for d in range(8) for c in range(2)],
                axis=0,
            )
            for hx in range(2)
        ],
        axis=1,
    )
    high, low = halves(picked)
    for n in range(8):
        chunk = lax.rem(me // 2 + n, 8)
        lanes = pl.ds(pl.multiple_of(chunk * 256, 256), 256)
        ones = lt[:, lanes]
        wide = (mm(high, ones) + mm(low, ones)).reshape(8, 32, 256)
        d_here = jnp.broadcast_to(sm_ref[0:1, lanes] & 7, (32, 256))
        total = wide[0]
        for d in range(1, 8):
            total = jnp.where(d_here == d, wide[d], total)
        for half in range(2):
            to = chunk * 2 + half
            for c in range(2):
                for orb in range(2):
                    s2[to, c * 8 : c * 8 + 8, orb * 128 : orb * 128 + 128] = total[
                        c * 16 + orb * 8 : c * 16 + orb * 8 + 8, half * 128 : half * 128 + 128
                    ]

            @pl.when(to != me)
            def _():
                b_copy(lax.rem(to - me + 16, 16)).start()

    r2[me] = s2[me]
    for k in range(1, 16):
        b_copy(k).wait_recv()

    high, low = halves(r2[...].reshape(256, 256))
    loads[5].wait()
    result = mm(zb[...], jnp.concatenate([high, high, low], axis=0)) * (2.0 / GRID**3)
    for orb in range(2):
        for c in range(2):
            o_ref[0, 2 * orb + c] = jnp.where(
                live, result[c * 72 : c * 72 + span, orb * 128 : orb * 128 + 128], 0.0
            )

    for k in range(1, n_z):
        gz_copy(k).wait_send()
    for k in range(1, n_y):
        gy_copy(k).wait_send()
    for k in range(1, 16):
        a_copy(k).wait_send()
        b_copy(k).wait_send()


def per_device(n_z, n_y, coeffs, potential, stick_map):
    consts = tables()
    vmem = pl.BlockSpec(memory_space=pltpu.VMEM)
    hbm = pl.BlockSpec(memory_space=pl.ANY)
    dma = pltpu.SemaphoreType.DMA
    scratch = [pltpu.VMEM(t.shape, BF) for t in consts] + [
        pltpu.VMEM((2, 80, 256), F32),
        pltpu.VMEM((16, 16, 256), F32),
        pltpu.VMEM((16, 16, 256), F32),
        pltpu.VMEM((16, 16, 256), F32),
        pltpu.VMEM((16, 16, 256), F32),
        pltpu.VMEM((n_y, n_z) + potential.shape, F32),
        pltpu.VMEM((256, 2048), BF),
        pltpu.VMEM((8, 16, 2048), BF),
        pltpu.VMEM((512, 2048), BF),
        pltpu.VMEM((2, 256, 128), F32),
        pltpu.VMEM((8, 240, 256), BF),
        pltpu.VMEM((2, 128, 512), F32),
        pltpu.VMEM((2, 128, 128), F32),
        pltpu.VMEM((2, 256, 128), F32),
        dma((len(consts),)),
        dma((16,)), dma((16,)), dma((16,)), dma((16,)),
        dma((4,)), dma((4,)), dma((4,)), dma((4,)), dma,
    ]
    return pl.pallas_call(
        functools.partial(kernel, n_z, n_y),
        out_shape=jax.ShapeDtypeStruct(coeffs.shape, F32),
        in_specs=[vmem, vmem, vmem] + [hbm] * len(consts),
        out_specs=vmem,
        scratch_shapes=scratch,
        compiler_params=pltpu.CompilerParams(
            collective_id=0, has_side_effects=True, vmem_limit_bytes=40 * 1024 * 1024
        ),
    )(coeffs, potential, stick_map, *[jnp.asarray(t) for t in consts])


def solution(mesh):
    n_band = mesh.shape["band"]
    n_z = 4 if n_band == 16 else 1
    placed = (P("band", None, None, "plane"), P("plane", "band", None), P())
    return jax.shard_map(
        functools.partial(per_device, n_z, n_band // n_z),
        mesh=mesh,
        in_specs=placed,
        out_specs=P("band", None, None, "plane"),
        check_vma=False,
    )
```

profile of v0, /device:TPU:225, one launch (start us, length us, event | category | flops | bytes accessed | tf_op | source)
XLA Modules:
  0.0 45.5 jit_solution(9532608562159937657)
XLA Ops:
  0.0 0.0 copy-start.2
  0.0 1.0 %copy.10.c_ref = f32[1,4,65,128]{3,2,1,0:T(8,128)S(1)} copy(f32[1,4,65,128]{3,1,2,0:T(4,128)} %param.9) | data formatting | bytes 266240 | tf_op args[0]
  1.0 0.0 copy-done.2
  1.0 0.0 copy-start
  1.0 1.1 %copy-done = bf16[1536,256]{1,0:T(8,128)(2,1)S(1)} copy-done((bf16[1536,256]{1,0:T(8,128)(2,1)S(1)}, bf16[1536,256]{1,0:T(8,128)(2,1)}, u32[]{:S(2)}) %copy-start) | copy-done | bytes 786456
  2.1 0.0 copy-start.1
  2.2 1.0 %copy-done.1 = bf16[2,384,256]{2,1,0:T(8,128)(2,1)S(1)} copy-done((bf16[2,384,256]{2,1,0:T(8,128)(2,1)S(1)}, bf16[2,384,256]{2,1,0:T(8,128)(2,1)}, u32[]{:S(2)}) %copy-start.1) | copy-done | bytes 393240
  3.1 0.0 copy-start.3
  3.1 0.9 %copy-done.3 = bf16[144,768]{1,0:T(8,128)(2,1)S(1)} copy-done((bf16[144,768]{1,0:T(8,128)(2,1)S(1)}, bf16[144,768]{1,0:T(8,128)(2,1)}, u32[]{:S(2)}) %copy-start.3) | copy-done | bytes 221208
  4.1 0.0 copy-start.4
  4.1 0.8 %copy-done.4 = bf16[128,240]{1,0:T(8,128)(2,1)S(1)} copy-done((bf16[128,240]{1,0:T(8,128)(2,1)S(1)}, bf16[128,240]{1,0:T(8,128)(2,1)}, u32[]{:S(2)}) %copy-start.4) | copy-done | bytes 61464
  4.9 0.0 copy-start.5
  4.9 0.8 %copy-done.5 = bf16[80,384]{1,0:T(8,128)(2,1)S(1)} copy-done((bf16[80,384]{1,0:T(8,128)(2,1)S(1)}, bf16[80,384]{1,0:T(8,128)(2,1)}, u32[]{:S(2)}) %copy-start.5) | copy-done | bytes 61464
  5.8 0.0 copy-start.6
  5.8 0.8 %copy-done.6 = f32[8,8,128]{2,1,0:T(8,128)S(1)} copy-done((f32[8,8,128]{2,1,0:T(8,128)S(1)}, f32[8,8,128]{2,1,0:T(8,128)}, u32[]{:S(2)}) %copy-start.6) | copy-done | bytes 32792
  6.5 0.0 copy-start.7
  6.5 0.8 %copy-done.7 = s32[3,2048]{1,0:T(4,128)S(1)} copy-done((s32[3,2048]{1,0:T(4,128)S(1)}, s32[3,2048]{1,0:T(4,128)}, u32[]{:S(2)}) %copy-start.7) | copy-done | bytes 24600
  7.3 37.5 %shard_map.91 = f32[1,4,65,128]{3,2,1,0:T(8,128)S(1)} custom-call(f32[1,4,65,128]{3,2,1,0:T(8,128)S(1)} %copy.10.c_ref, f32[8,8,128]{2,1,0:T(8,128)S(1)} %copy-done.6, s32[3,2048]{1,0:T(4,128)S(1)} %copy-done.7, bf16[256,480]{1,0:T(8,128)(2,1)S(1)} %copy-done.2, bf16[2,384,256]{2,1,0:T(8,128)(2,1)S(1)} %copy-done.1, bf16[128,240]{1,0:T(8,128)(2,1)S(1)} %copy-done.4, ...), custom_call_target="tpu_custom_call" | custom-call | tf_op jit(solution)/shard_map/pallas_call | solution.py:351
  44.8 0.7 %copy.11 = f32[1,4,65,128]{3,1,2,0:T(4,128)} copy(f32[1,4,65,128]{3,2,1,0:T(8,128)S(1)} %shard_map.91) | data formatting | bytes 266240 | tf_op jit(solution)/shard_map/pallas_call | solution.py:351
Async XLA Ops:
  0.0 1.0 %copy-start.2 = (bf16[256,480]{1,0:T(8,128)(2,1)S(1)}, bf16[256,480]{1,0:T(8,128)(2,1)}, u32[]{:S(2)}) copy-start(bf16[256,480]{1,0:T(8,128)(2,1)} %constant.12.clone.zf_h) | copy-start | bytes 737284
  1.0 1.1 %copy-start = (bf16[1536,256]{1,0:T(8,128)(2,1)S(1)}, bf16[1536,256]{1,0:T(8,128)(2,1)}, u32[]{:S(2)}) copy-start(bf16[1536,256]{1,0:T(8,128)(2,1)} %constant.16.clone.wb_h) | copy-start | bytes 2359300
  2.1 1.0 %copy-start.1 = (bf16[2,384,256]{2,1,0:T(8,128)(2,1)S(1)}, bf16[2,384,256]{2,1,0:T(8,128)(2,1)}, u32[]{:S(2)}) copy-start(bf16[2,384,256]{2,1,0:T(8,128)(2,1)} %constant.13.clone.wy_h) | copy-start | bytes 1179652
  3.1 0.9 %copy-start.3 = (bf16[144,768]{1,0:T(8,128)(2,1)S(1)}, bf16[144,768]{1,0:T(8,128)(2,1)}, u32[]{:S(2)}) copy-start(bf16[144,768]{1,0:T(8,128)(2,1)} %constant.17.clone.zb_h) | copy-start | bytes 663556
  4.1 0.8 %copy-start.4 = (bf16[128,240]{1,0:T(8,128)(2,1)S(1)}, bf16[128,240]{1,0:T(8,128)(2,1)}, u32[]{:S(2)}) copy-start(bf16[128,240]{1,0:T(8,128)(2,1)} %constant.14.clone.xf_h) | copy-start | bytes 184324
  4.9 0.8 %copy-start.5 = (bf16[80,384]{1,0:T(8,128)(2,1)S(1)}, bf16[80,384]{1,0:T(8,128)(2,1)}, u32[]{:S(2)}) copy-start(bf16[80,384]{1,0:T(8,128)(2,1)} %constant.15.clone.xb_h) | copy-start | bytes 184324
  5.8 0.8 %copy-start.6 = (f32[8,8,128]{2,1,0:T(8,128)S(1)}, f32[8,8,128]{2,1,0:T(8,128)}, u32[]{:S(2)}) copy-start(f32[8,8,128]{2,1,0:T(8,128)} %p_ref.1) | copy-start | bytes 98308
  6.5 0.8 %copy-start.7 = (s32[3,2048]{1,0:T(4,128)S(1)}, s32[3,2048]{1,0:T(4,128)}, u32[]{:S(2)}) copy-start(s32[3,2048]{1,0:T(4,128)} %sm_ref.1) | copy-start | bytes 73732
where the time goes:
time: 45.9 us; the launch traced here: 45.5 us
  Pallas kernels  37.5 us (82%)
  local copies, waits for them, and re-layouts  7.95 us (17%)
    pallas_call x1, Pallas kernels, per_device(): pl.pallas_call(functools.partial(kernel, n_z, n_y), out_shape=jax.ShapeDt...  37.5 us
    unnamed x17, local copies, waits for them, and re-layouts  7.26 us

commit v1 on v0

v1 whole, which is shorter than its diff:
```python
import functools

import jax
import jax.numpy as jnp
import ml_dtypes
import numpy as np
from jax import lax
from jax.experimental import pallas as pl
from jax.experimental.pallas import tpu as pltpu
from jax.sharding import PartitionSpec as P

MESH = pl.DeviceIdType.MESH
GRID = 128
RADIUS = 32
BF = jnp.bfloat16
F32 = jnp.float32


def _halves(table):
    high = table.astype(ml_dtypes.bfloat16)
    low = (table - high.astype(np.float64)).astype(ml_dtypes.bfloat16)
    return high, low


def _left(table):
    high, low = _halves(table)
    return np.concatenate([high, low, high], axis=1)


def _right(table):
    high, low = _halves(table)
    return np.concatenate([high, low, high], axis=0)


def _trig(left, right):
    turns = np.mod(np.outer(left, right), GRID) * (2.0 * np.pi / GRID)
    return np.cos(turns), np.sin(turns)


def tables():
    points = np.arange(GRID)
    depth = np.arange(2 * RADIUS + 1) - RADIUS
    span = depth.size
    cos, sin = _trig(points, depth)
    zf = np.zeros((16, 2, 8, 2, 80))
    cos, sin = cos.reshape(16, 8, span), sin.reshape(16, 8, span)
    zf[:, 0, :, 0, :span], zf[:, 0, :, 1, :span] = cos, -sin
    zf[:, 1, :, 0, :span], zf[:, 1, :, 1, :span] = sin, cos
    zf = zf.reshape(16, 2, 2, 4, 160).transpose(2, 0, 1, 3, 4)
    zf = _left(zf.reshape(256, 160))
    zb = np.zeros((2, 72, 16, 2, 8))
    cos, sin = np.moveaxis(cos, 2, 0), np.moveaxis(sin, 2, 0)
    zb[0, :span, :, 0], zb[0, :span, :, 1] = cos, sin
    zb[1, :span, :, 0], zb[1, :span, :, 1] = -sin, cos
    zb = zb.reshape(144, 16, 2, 2, 4).transpose(0, 3, 1, 2, 4).reshape(144, 2, 128)
    zb = np.stack([_left(zb[:, h]) for h in range(2)])
    cos, sin = _trig(np.arange(64) - 31, points)
    wy = np.zeros((2, 2, 64, 2, GRID))
    wb = np.zeros((2, 2, GRID, 2, 2, 64))
    for i in range(2):
        wy[i, i, :, 0], wy[i, i, :, 1] = cos, sin
        wb[i, 0, :, 0, i], wb[i, 1, :, 0, i] = cos.T, sin.T
        wb[i, 0, :, 1, i], wb[i, 1, :, 1, i] = -sin.T, cos.T
    wy = np.stack([_right(wy[i].reshape(128, 256)) for i in range(2)])
    wb = _right(wb.reshape(512, 256))
    cos, sin = _trig(np.arange(32), points)
    base = np.zeros((5, 2, 8, GRID))
    base[:4, 0], base[:4, 1] = cos.reshape(4, 8, GRID), -sin.reshape(4, 8, GRID)
    cos, sin = _trig(np.array([RADIUS]), points)
    base[4, 0, 0], base[4, 1, 0] = cos[0] - 1.0, -sin[0]
    base = base.reshape(80, GRID)
    xf, xb = _left(base.T), _left(base)
    return zf, wy, xf, xb, wb, zb


def halves(value):
    high = value.astype(BF)
    return high, (value - high.astype(F32)).astype(BF)


def mm(left, right):
    return jnp.dot(left, right, preferred_element_type=F32)


OFFSETS = [(dx, dz, dc) for dz in (1, 0) for dx in (2, 1, 3, 0) for dc in (1, 0)]
PEERS = [o for o in OFFSETS if o != (0, 0, 0)]
CHUNKS = [o for o in OFFSETS if o[2] == 0]


def kernel(
    n_z, n_y,
    c_h, p_h, sm_h, zf_h, wy_h, xf_h, xb_h, wb_h, zb_h,
    o_ref,
    c_ref, sm_ref, zf, wy, xf, xb, wb, zb,
    xs, zs, r1, s2, r2, slab, lt, dm, m1, gs, bs, cs, sp, og,
    c_sem, a_s, a_r, b_s, b_r, gz_s, gz_r, gy_s, gy_r, own_sem,
):
    band = lax.axis_index("band")
    me = lax.axis_index("plane")
    z_me, y_me = band // n_y, lax.rem(band, n_y)
    x_at, half_at, core_at = me // 4, lax.rem(me // 2, 2), lax.rem(me, 2)
    span = c_ref.shape[0]

    def plane_peer(offset, sign=1):
        dx, dz, dc = offset
        return (
            lax.rem(x_at + sign * dx + 4, 4) * 4
            + lax.rem(half_at + dz, 2) * 2
            + lax.rem(core_at + dc, 2)
        )

    def z_peer(k):
        return lax.rem(z_me + k, n_z) * n_y + y_me

    def y_peer(k):
        return z_me * n_y + lax.rem(y_me + k, n_y)

    barrier = pltpu.get_barrier_semaphore()
    for o in PEERS:
        pl.semaphore_signal(
            barrier, inc=1, device_id={"plane": plane_peer(o)}, device_id_type=MESH
        )
    for k in range(1, n_z):
        pl.semaphore_signal(barrier, inc=1, device_id={"band": z_peer(k)}, device_id_type=MESH)
    for k in range(1, n_y):
        pl.semaphore_signal(barrier, inc=1, device_id={"band": y_peer(k)}, device_id_type=MESH)

    loads = [
        pltpu.make_async_copy(src, dst, c_sem.at[n])
        for n, (src, dst) in enumerate(
            [
                (c_h, c_ref), (sm_h, sm_ref), (zf_h, zf), (wy_h, wy),
                (xf_h, xf), (xb_h, xb), (wb_h, wb), (zb_h, zb),
            ]
        )
    ]
    for load in loads[:3]:
        load.start()

    def a_copy(h, n):
        to = plane_peer(PEERS[n])
        return pltpu.make_async_remote_copy(
            src_ref=zs.at[h, to], dst_ref=r1.at[h, me],
            send_sem=a_s.at[h, n], recv_sem=a_r.at[h, n],
            device_id={"plane": to}, device_id_type=MESH,
        )

    def b_copy(h, n):
        to = plane_peer(PEERS[n])
        return pltpu.make_async_remote_copy(
            src_ref=s2.at[h, to], dst_ref=r2.at[h, me],
            send_sem=b_s.at[h, n], recv_sem=b_r.at[h, n],
            device_id={"plane": to}, device_id_type=MESH,
        )

    def gz_copy(h, k):
        return pltpu.make_async_remote_copy(
            src_ref=p_h.at[pl.ds(h * 4, 4)], dst_ref=slab.at[h, y_me, z_me],
            send_sem=gz_s.at[h, k], recv_sem=gz_r.at[h, k],
            device_id={"band": z_peer(k)}, device_id_type=MESH,
        )

    def gy_copy(h, back, k):
        z_from = lax.rem(z_me - back + n_z, n_z)
        own = p_h.at[pl.ds(h * 4, 4)]
        return pltpu.make_async_remote_copy(
            src_ref=slab.at[h, y_me, z_from] if back else own, dst_ref=slab.at[h, y_me, z_from],
            send_sem=gy_s.at[h, back, k], recv_sem=gy_r.at[h, back, k],
            device_id={"band": y_peer(k)}, device_id_type=MESH,
        )

    def own_copy(h):
        return pltpu.make_async_copy(
            p_h.at[pl.ds(h * 4, 4)], slab.at[h, y_me, z_me], own_sem.at[h]
        )

    def gather_start(h):
        for k in range(1, n_z):
            gz_copy(h, k).start()
        for k in range(1, n_y):
            gy_copy(h, 0, k).start()

    pl.semaphore_wait(barrier, 15 + n_z - 1 + n_y - 1)
    gather_start(0)

    loads[0].wait()
    loads[1].wait()
    heights = sm_ref[2:3, pl.ds(pl.multiple_of(me * 128, 128), 128)]
    live = jnp.abs(lax.broadcasted_iota(jnp.int32, (span, 128), 0) - RADIUS) <= heights
    xs[:, 64:80, :] = jnp.zeros((2, 16, 256), F32)
    for orb in range(2):
        for c in range(2):
            xs[c, 0:span, orb * 128 : orb * 128 + 128] = jnp.where(
                live, c_ref[:, 2 * orb + c, :], 0.0
            )
    high, low = halves(xs[...].reshape(160, 256))
    stacked = jnp.concatenate([high, high, low], axis=0)
    loads[2].wait()
    for h in range(2):
        zs[h] = mm(zf[h * 128 : h * 128 + 128], stacked).reshape(16, 8, 256)
        for n in range(15):
            a_copy(h, n).start()
        if h == 0:
            gather_start(1)
    for load in loads[3:]:
        load.start()
    for h in range(2):
        own_copy(h).start()
        r1[h, me] = zs[h, me]

    stick_x, stick_y = sm_ref[0:1, :], sm_ref[1:2, :]
    d_of = stick_x & 7
    lane_of = ((stick_x >> 3) & 3) * 64 + stick_y + 31
    for n in range(16):
        rows = lax.broadcasted_iota(jnp.int32, (16, 2048), 0) + n * 16
        lt[n * 16 : n * 16 + 16, :] = jnp.where(rows == lane_of, 1.0, 0.0).astype(BF)
    for n in range(4):
        rows = lax.broadcasted_iota(jnp.int32, (16, 2048), 0) // 8 + n * 2
        dm[n] = jnp.where(rows == d_of, 1.0, 0.0).astype(BF)

    for h in range(2):
        for back in sorted(range(1, n_z), key=lambda k: min(k, n_z - k)):
            gz_copy(h, back).wait_recv()
            for k in range(1, n_y):
                gy_copy(h, back, k).start()

    at_zero = lax.broadcasted_iota(jnp.int32, (64, 128), 1) == 31

    def place(h, source):
        lanes = pl.ds(pl.multiple_of(source * 128, 128), 128)
        block = r1[h, source]
        twice = jnp.concatenate([block, block], axis=0)
        for p, part in enumerate(halves(twice)):
            for orb in range(2):
                piece = part[:, orb * 128 : orb * 128 + 128]
                for n in range(4):
                    at = p * 128 + orb * 64 + n * 16
                    m1[h, at : at + 16, lanes] = piece * dm[n, :, lanes]

    def keep(h, value, at):
        high, low = halves(value)
        for orb in range(2):
            lanes = slice(orb * 128, orb * 128 + 128)
            bs[h, :, at : at + 16, lanes] = high[orb]
            bs[h, :, 80 + at : 96 + at, lanes] = high[orb]
            bs[h, :, 160 + at : 176 + at, lanes] = low[orb]

    def middle(h):
        place(h, me)
        for n in reversed(range(15)):
            a_copy(h, n).wait_recv()
            place(h, plane_peer(PEERS[n], -1))
        both = lax.dot_general(
            m1[h], lt[...], (((1,), (1,)), ((), ())), preferred_element_type=F32
        )
        both = both[:128] + both[128:]
        for hx in range(2):
            gs[h, hx] = both[:, hx * 128 : hx * 128 + 128]
        grid = [
            jnp.concatenate(
                [
                    gs[h, hx, pl.ds(orb * 64 + c * 4 + z, 8, stride=8), :]
                    for orb in range(2)
                    for z in range(4)
                    for c in range(2)
                ],
                axis=0,
            )
            for hx in range(2)
        ]

        if h == 0:
            loads[3].wait()
        for hx in range(2):
            high, low = halves(grid[hx])
            left = jnp.concatenate([high, high, low], axis=1)
            for i in range(2):
                turned = mm(left, wy[i]).reshape(2, 4, 2, 8, 256)
                real = turned[:, :, 0, :, :128] - turned[:, :, 1, :, 128:]
                imag = turned[:, :, 0, :, 128:] + turned[:, :, 1, :, :128]
                keep(h, jnp.concatenate([real, imag], axis=2), (2 * hx + i) * 16)
        keep(h, jnp.broadcast_to(grid[0][:, 31:32], (128, 128)).reshape(2, 4, 16, 128), 64)

        own_copy(h).wait()
        for back in range(n_z):
            for k in range(1, n_y):
                gy_copy(h, back, k).wait_recv()
        if h == 0:
            loads[4].wait()
            loads[5].wait()

        for z in range(4):
            field = mm(xf[...], bs[h, z])
            plane = jnp.concatenate(
                [slab[h, b % n_y, b // n_y, z] for b in range(n_z * n_y)], axis=0
            )
            high, low = halves(field * jnp.concatenate([plane, plane], axis=1))
            back = mm(xb[...], jnp.concatenate([high, high, low], axis=0))
            for orb in range(2):
                lanes = slice(orb * 128, orb * 128 + 128)
                rows = slice(orb * 32 + z * 8, orb * 32 + z * 8 + 8)
                for xl in range(4):
                    for c in range(2):
                        at = ((xl % 2) * 2 + c) * 128
                        cs[h, xl // 2, rows, at : at + 128] = back[
                            (xl * 2 + c) * 8 : (xl * 2 + c) * 8 + 8, lanes
                        ]
                for c in range(2):
                    sp[h, c, rows, :] = back[64 + c * 8 : 72 + c * 8, lanes]

        if h == 0:
            loads[6].wait()
        for hx in range(2):
            high, low = halves(cs[h, hx])
            turned = mm(jnp.concatenate([high, high, low], axis=1), wb[...])
            for c in range(2):
                part = turned[:, c * 128 : c * 128 + 128]
                if hx == 0:
                    extra = jnp.sum(sp[h, c], axis=1, keepdims=True)
                    part = part + jnp.where(at_zero, extra, 0.0)
                for orb in range(2):
                    at = orb * 64 + c * 32
                    og[h, hx, at : at + 32, :] = part[orb * 32 : orb * 32 + 32]

        picked = jnp.concatenate(
            [
                jnp.concatenate(
                    [
                        og[h, hx, pl.ds(orb * 64 + d, 8, stride=8), :]
                        for d in range(8)
                        for orb in range(2)
                    ],
                    axis=0,
                )
                for hx in range(2)
            ],
            axis=1,
        )
        high, low = halves(picked)
        for chunk_offset in CHUNKS:
            chunk = plane_peer(chunk_offset) // 2
            lanes = pl.ds(pl.multiple_of(chunk * 256, 256), 256)
            ones = lt[:, lanes]
            wide = (mm(high, ones) + mm(low, ones)).reshape(8, 16, 256)
            d_here = jnp.broadcast_to(sm_ref[0:1, lanes] & 7, (16, 256))
            total = wide[0]
            for d in range(1, 8):
                total = jnp.where(d_here == d, wide[d], total)
            for core in range(2):
                for orb in range(2):
                    s2[h, chunk * 2 + core, :, orb * 128 : orb * 128 + 128] = total[
                        orb * 8 : orb * 8 + 8, core * 128 : core * 128 + 128
                    ]
            for n, o in enumerate(PEERS):
                if o[:2] == chunk_offset[:2]:
                    b_copy(h, n).start()
        r2[h, me] = s2[h, me]

    middle(0)
    middle(1)

    for h in range(2):
        for k in range(1, n_z):
            gz_copy(h, k).wait_send()
        for back in range(n_z):
            for k in range(1, n_y):
                gy_copy(h, back, k).wait_send()
        for n in range(15):
            a_copy(h, n).wait_send()
    loads[7].wait()
    result = None
    for h in range(2):
        for n in range(15):
            b_copy(h, n).wait_send()
        for n in range(15):
            b_copy(h, n).wait_recv()
        high, low = halves(r2[h].reshape(128, 256))
        part = mm(zb[h], jnp.concatenate([high, high, low], axis=0))
        result = part if h == 0 else result + part
    result = result * (2.0 / GRID**3)
    for orb in range(2):
        for c in range(2):
            o_ref[:, 2 * orb + c, :] = jnp.where(
                live, result[c * 72 : c * 72 + span, orb * 128 : orb * 128 + 128], 0.0
            )


def per_device(n_z, n_y, coeffs, potential, stick_map):
    consts = tables()
    moved = jnp.transpose(coeffs[0], (1, 0, 2))
    vmem = pl.BlockSpec(memory_space=pltpu.VMEM)
    hbm = pl.BlockSpec(memory_space=pltpu.HBM)
    dma = pltpu.SemaphoreType.DMA
    scratch = [
        pltpu.VMEM(moved.shape, F32),
        pltpu.VMEM(stick_map.shape, jnp.int32),
    ] + [pltpu.VMEM(t.shape, BF) for t in consts] + [
        pltpu.VMEM((2, 80, 256), F32),
        pltpu.VMEM((2, 16, 8, 256), F32),
        pltpu.VMEM((2, 16, 8, 256), F32),
        pltpu.VMEM((2, 16, 8, 256), F32),
        pltpu.VMEM((2, 16, 8, 256), F32),
        pltpu.VMEM((2, n_y, n_z, 4) + potential.shape[1:], F32),
        pltpu.VMEM((256, 2048), BF),
        pltpu.VMEM((4, 16, 2048), BF),
        pltpu.VMEM((2, 256, 2048), BF),
        pltpu.VMEM((2, 2, 128, 128), F32),
        pltpu.VMEM((2, 4, 240, 256), BF),
        pltpu.VMEM((2, 2, 64, 512), F32),
        pltpu.VMEM((2, 2, 64, 128), F32),
        pltpu.VMEM((2, 2, 128, 128), F32),
        dma((len(consts) + 2,)),
        dma((2, 16)), dma((2, 16)), dma((2, 16)), dma((2, 16)),
        dma((2, 4)), dma((2, 4)), dma((2, 4, 4)), dma((2, 4, 4)), dma((2,)),
    ]
    result = pl.pallas_call(
        functools.partial(kernel, n_z, n_y),
        out_shape=jax.ShapeDtypeStruct(moved.shape, F32),
        in_specs=[hbm] * (len(consts) + 3),
        out_specs=vmem,
        scratch_shapes=scratch,
        compiler_params=pltpu.CompilerParams(
            collective_id=0, has_side_effects=True, vmem_limit_bytes=40 * 1024 * 1024
        ),
    )(
        *[
            pltpu.with_memory_space_constraint(value, pltpu.HBM)
            for value in (moved, potential, stick_map, *[jnp.asarray(t) for t in consts])
        ]
    )
    return jnp.transpose(result, (1, 0, 2))[None]


def solution(mesh):
    n_band = mesh.shape["band"]
    n_z = 4 if n_band == 16 else 1
    placed = (P("band", None, None, "plane"), P("plane", "band", None), P())
    return jax.shard_map(
        functools.partial(per_device, n_z, n_band // n_z),
        mesh=mesh,
        in_specs=placed,
        out_specs=P("band", None, None, "plane"),
        check_vma=False,
    )
```

time: 45.9 us -> 36.8 us (0.80)
  the two profiles are of different devices: /device:TPU:225 before, /device:TPU:32 now
where the time goes in v1:
time: 36.8 us
  Pallas kernels  36.1 us (98%)
  local copies, waits for them, and re-layouts  0.66 us (2%)
    pallas_call x1, Pallas kernels, per_device(): pl.pallas_call(functools.partial(kernel, n_z, n_y), out_shape=jax.ShapeDt...  36.1 us

profile of v1, /device:TPU:32, one launch (start us, length us, event | category | flops | bytes accessed | tf_op | source)
XLA Modules:
  0.0 36.8 jit_solution(12790820397590714002)
XLA Ops:
  0.0 36.1 %shard_map.91 = f32[65,4,128]{2,1,0:T(4,128)S(1)} custom-call(f32[65,4,128]{2,1,0:T(4,128)} %bitcast.7, f32[8,8,128]{2,1,0:T(8,128)} %p_h.1, s32[3,2048]{1,0:T(4,128)} %sm_h.1, bf16[256,480]{1,0:T(8,128)(2,1)} %constant.12.clone.zf_h, bf16[2,384,256]{2,1,0:T(8,128)(2,1)} %constant.13.clone.wy_h, bf16[128,240]{1,0:T(8,128)(2,1)} %constant.14.clone.xf_h, ...), custom_call_target="tpu_custom_call" | custom-call | tf_op jit(solution)/shard_map/pallas_call | solution.py:416
  36.1 0.7 %copy.11 = f32[1,4,65,128]{3,1,2,0:T(4,128)} copy(f32[1,4,65,128]{3,1,2,0:T(4,128)S(1)} %bitcast.6) | data formatting | bytes 266240

commit v2 on v1

--- a/solution.py
+++ b/solution.py
@@ -83,7 +83,6 @@
 
 
 OFFSETS = [(dx, dz, dc) for dz in (1, 0) for dx in (2, 1, 3, 0) for dc in (1, 0)]
-PEERS = [o for o in OFFSETS if o != (0, 0, 0)]
 CHUNKS = [o for o in OFFSETS if o[2] == 0]
 
 
@@ -109,21 +108,18 @@
             + lax.rem(core_at + dc, 2)
         )
 
+    side = lax.rem(z_me, 2)
+    partner = [
+        lax.rem(z_me + 2, n_z) * n_y + y_me,
+        (z_me + 1 - 2 * side) * n_y + y_me,
+    ]
+    half_of = [side, 1 - side]
+
     def z_peer(k):
         return lax.rem(z_me + k, n_z) * n_y + y_me
 
     def y_peer(k):
         return z_me * n_y + lax.rem(y_me + k, n_y)
-
-    barrier = pltpu.get_barrier_semaphore()
-    for o in PEERS:
-        pl.semaphore_signal(
-            barrier, inc=1, device_id={"plane": plane_peer(o)}, device_id_type=MESH
-        )
-    for k in range(1, n_z):
-        pl.semaphore_signal(barrier, inc=1, device_id={"band": z_peer(k)}, device_id_type=MESH)
-    for k in range(1, n_y):
-        pl.semaphore_signal(barrier, inc=1, device_id={"band": y_peer(k)}, device_id_type=MESH)
 
     loads = [
         pltpu.make_async_copy(src, dst, c_sem.at[n])
@@ -137,51 +133,60 @@
     for load in loads[:3]:
         load.start()
 
+    barrier = pltpu.get_barrier_semaphore()
+    for band_to in partner:
+        for o in OFFSETS:
+            pl.semaphore_signal(
+                barrier, inc=1,
+                device_id={"band": band_to, "plane": plane_peer(o)}, device_id_type=MESH,
+            )
+    last = lax.rem(z_me + 3 - 2 * side + n_z, n_z) * n_y + y_me
+    pl.semaphore_signal(barrier, inc=1, device_id={"band": last}, device_id_type=MESH)
+    for k in range(1, n_y):
+        pl.semaphore_signal(barrier, inc=1, device_id={"band": y_peer(k)}, device_id_type=MESH)
+
     def a_copy(h, n):
-        to = plane_peer(PEERS[n])
+        to = plane_peer(OFFSETS[n])
         return pltpu.make_async_remote_copy(
-            src_ref=zs.at[h, to], dst_ref=r1.at[h, me],
+            src_ref=zs.at[half_of[h], to], dst_ref=r1.at[h, me],
             send_sem=a_s.at[h, n], recv_sem=a_r.at[h, n],
-            device_id={"plane": to}, device_id_type=MESH,
+            device_id={"band": partner[h], "plane": to}, device_id_type=MESH,
         )
 
     def b_copy(h, n):
-        to = plane_peer(PEERS[n])
+        to = plane_peer(OFFSETS[n])
         return pltpu.make_async_remote_copy(
-            src_ref=s2.at[h, to], dst_ref=r2.at[h, me],
+            src_ref=s2.at[h, to], dst_ref=r2.at[side, me],
             send_sem=b_s.at[h, n], recv_sem=b_r.at[h, n],
-            device_id={"plane": to}, device_id_type=MESH,
-        )
-
-    def gz_copy(h, k):
+            device_id={"band": partner[h], "plane": to}, device_id_type=MESH,
+        )
+
+    def gz_copy(k):
+        at = lax.rem(z_me + k, 2) * 4
         return pltpu.make_async_remote_copy(
-            src_ref=p_h.at[pl.ds(h * 4, 4)], dst_ref=slab.at[h, y_me, z_me],
-            send_sem=gz_s.at[h, k], recv_sem=gz_r.at[h, k],
+            src_ref=p_h.at[pl.ds(at, 4)], dst_ref=slab.at[y_me, z_me],
+            send_sem=gz_s.at[k], recv_sem=gz_r.at[k],
             device_id={"band": z_peer(k)}, device_id_type=MESH,
         )
 
-    def gy_copy(h, back, k):
+    def gy_copy(back, k):
         z_from = lax.rem(z_me - back + n_z, n_z)
-        own = p_h.at[pl.ds(h * 4, 4)]
+        own = p_h.at[pl.ds(side * 4, 4)]
         return pltpu.make_async_remote_copy(
-            src_ref=slab.at[h, y_me, z_from] if back else own, dst_ref=slab.at[h, y_me, z_from],
-            send_sem=gy_s.at[h, back, k], recv_sem=gy_r.at[h, back, k],
+            src_ref=slab.at[y_me, z_from] if back else own, dst_ref=slab.at[y_me, z_from],
+            send_sem=gy_s.at[back, k], recv_sem=gy_r.at[back, k],
             device_id={"band": y_peer(k)}, device_id_type=MESH,
         )
 
-    def own_copy(h):
-        return pltpu.make_async_copy(
-            p_h.at[pl.ds(h * 4, 4)], slab.at[h, y_me, z_me], own_sem.at[h]
-        )
-
-    def gather_start(h):
-        for k in range(1, n_z):
-            gz_copy(h, k).start()
-        for k in range(1, n_y):
-            gy_copy(h, 0, k).start()
-
-    pl.semaphore_wait(barrier, 15 + n_z - 1 + n_y - 1)
-    gather_start(0)
+    own_copy = pltpu.make_async_copy(
+        p_h.at[pl.ds(side * 4, 4)], slab.at[y_me, z_me], own_sem
+    )
+
+    pl.semaphore_wait(barrier, 33 + n_y - 1)
+    for k in range(1, n_z):
+        gz_copy(k).start()
+    for k in range(1, n_y):
+        gy_copy(0, k).start()
 
     loads[0].wait()
     loads[1].wait()
@@ -197,16 +202,14 @@
     stacked = jnp.concatenate([high, high, low], axis=0)
     loads[2].wait()
     for h in range(2):
-        zs[h] = mm(zf[h * 128 : h * 128 + 128], stacked).reshape(16, 8, 256)
-        for n in range(15):
+        zs[half_of[h]] = mm(
+            zf[pl.ds(pl.multiple_of(half_of[h] * 128, 128), 128), :], stacked
+        ).reshape(16, 8, 256)
+        for n in range(16):
             a_copy(h, n).start()
-        if h == 0:
-            gather_start(1)
     for load in loads[3:]:
         load.start()
-    for h in range(2):
-        own_copy(h).start()
-        r1[h, me] = zs[h, me]
+    own_copy.start()
 
     stick_x, stick_y = sm_ref[0:1, :], sm_ref[1:2, :]
     d_of = stick_x & 7
@@ -218,11 +221,10 @@
         rows = lax.broadcasted_iota(jnp.int32, (16, 2048), 0) // 8 + n * 2
         dm[n] = jnp.where(rows == d_of, 1.0, 0.0).astype(BF)
 
-    for h in range(2):
-        for back in sorted(range(1, n_z), key=lambda k: min(k, n_z - k)):
-            gz_copy(h, back).wait_recv()
-            for k in range(1, n_y):
-                gy_copy(h, back, k).start()
+    for back in sorted(range(1, n_z), key=lambda k: min(k, n_z - k)):
+        gz_copy(back).wait_recv()
+        for k in range(1, n_y):
+            gy_copy(back, k).start()
 
     at_zero = lax.broadcasted_iota(jnp.int32, (64, 128), 1) == 31
 
@@ -245,11 +247,10 @@
             bs[h, :, 80 + at : 96 + at, lanes] = high[orb]
             bs[h, :, 160 + at : 176 + at, lanes] = low[orb]
 
-    def middle(h):
-        place(h, me)
-        for n in reversed(range(15)):
+    def to_columns(h):
+        for n in reversed(range(16)):
             a_copy(h, n).wait_recv()
-            place(h, plane_peer(PEERS[n], -1))
+            place(h, plane_peer(OFFSETS[n], -1))
         both = lax.dot_general(
             m1[h], lt[...], (((1,), (1,)), ((), ())), preferred_element_type=F32
         )
@@ -281,18 +282,19 @@
                 keep(h, jnp.concatenate([real, imag], axis=2), (2 * hx + i) * 16)
         keep(h, jnp.broadcast_to(grid[0][:, 31:32], (128, 128)).reshape(2, 4, 16, 128), 64)
 
-        own_copy(h).wait()
-        for back in range(n_z):
-            for k in range(1, n_y):
-                gy_copy(h, back, k).wait_recv()
+    def through_planes(h):
         if h == 0:
+            own_copy.wait()
+            for back in range(n_z):
+                for k in range(1, n_y):
+                    gy_copy(back, k).wait_recv()
             loads[4].wait()
             loads[5].wait()
 
         for z in range(4):
             field = mm(xf[...], bs[h, z])
             plane = jnp.concatenate(
-                [slab[h, b % n_y, b // n_y, z] for b in range(n_z * n_y)], axis=0
+                [slab[b % n_y, b // n_y, z] for b in range(n_z * n_y)], axis=0
             )
             high, low = halves(field * jnp.concatenate([plane, plane], axis=1))
             back = mm(xb[...], jnp.concatenate([high, high, low], axis=0))
@@ -351,31 +353,32 @@
                     s2[h, chunk * 2 + core, :, orb * 128 : orb * 128 + 128] = total[
                         orb * 8 : orb * 8 + 8, core * 128 : core * 128 + 128
                     ]
-            for n, o in enumerate(PEERS):
+            for n, o in enumerate(OFFSETS):
                 if o[:2] == chunk_offset[:2]:
                     b_copy(h, n).start()
-        r2[h, me] = s2[h, me]
-
-    middle(0)
-    middle(1)
-
+
+    to_columns(0)
+    to_columns(1)
+    through_planes(0)
+    through_planes(1)
+
+    for k in range(1, n_z):
+        gz_copy(k).wait_send()
+    for back in range(n_z):
+        for k in range(1, n_y):
+            gy_copy(back, k).wait_send()
     for h in range(2):
-        for k in range(1, n_z):
-            gz_copy(h, k).wait_send()
-        for back in range(n_z):
-            for k in range(1, n_y):
-                gy_copy(h, back, k).wait_send()
-        for n in range(15):
+        for n in range(16):
             a_copy(h, n).wait_send()
     loads[7].wait()
     result = None
     for h in range(2):
-        for n in range(15):
+        for n in range(16):
             b_copy(h, n).wait_send()
-        for n in range(15):
+        for n in range(16):
             b_copy(h, n).wait_recv()
-        high, low = halves(r2[h].reshape(128, 256))
-        part = mm(zb[h], jnp.concatenate([high, high, low], axis=0))
+        high, low = halves(r2[half_of[h]].reshape(128, 256))
+        part = mm(zb[half_of[h]], jnp.concatenate([high, high, low], axis=0))
         result = part if h == 0 else result + part
     result = result * (2.0 / GRID**3)
     for orb in range(2):
@@ -400,7 +403,7 @@
         pltpu.VMEM((2, 16, 8, 256), F32),
         pltpu.VMEM((2, 16, 8, 256), F32),
         pltpu.VMEM((2, 16, 8, 256), F32),
-        pltpu.VMEM((2, n_y, n_z, 4) + potential.shape[1:], F32),
+        pltpu.VMEM((n_y, n_z, 4) + potential.shape[1:], F32),
         pltpu.VMEM((256, 2048), BF),
         pltpu.VMEM((4, 16, 2048), BF),
         pltpu.VMEM((2, 256, 2048), BF),
@@ -411,7 +414,7 @@
         pltpu.VMEM((2, 2, 128, 128), F32),
         dma((len(consts) + 2,)),
         dma((2, 16)), dma((2, 16)), dma((2, 16)), dma((2, 16)),
-        dma((2, 4)), dma((2, 4)), dma((2, 4, 4)), dma((2, 4, 4)), dma((2,)),
+        dma((4,)), dma((4,)), dma((4, 4)), dma((4, 4)), dma,
     ]
     result = pl.pallas_call(
         functools.partial(kernel, n_z, n_y),

time: 36.8 us -> 34.4 us (0.935)
  the two profiles are of different devices: /device:TPU:32 before, /device:TPU:1 now
where the time goes in v2:
time: 34.4 us; the launch traced here: 34.3 us
  Pallas kernels  33.7 us (98%)
  local copies, waits for them, and re-layouts  0.66 us (2%)
    pallas_call x1, Pallas kernels, per_device(): pl.pallas_call(functools.partial(kernel, n_z, n_y), out_shape=jax.ShapeDt...  33.7 us

profile of v2, /device:TPU:1, one launch (start us, length us, event | category | flops | bytes accessed | tf_op | source)
XLA Modules:
  0.0 34.3 jit_solution(17780276652321670424)
XLA Ops:
  0.0 33.7 %shard_map.91 = f32[65,4,128]{2,1,0:T(4,128)S(1)} custom-call(f32[65,4,128]{2,1,0:T(4,128)} %bitcast.7, f32[8,8,128]{2,1,0:T(8,128)} %p_h.1, s32[3,2048]{1,0:T(4,128)} %sm_h.1, bf16[256,480]{1,0:T(8,128)(2,1)} %constant.12.clone.zf_h, bf16[2,384,256]{2,1,0:T(8,128)(2,1)} %constant.13.clone.wy_h, bf16[128,240]{1,0:T(8,128)(2,1)} %constant.14.clone.xf_h, ...), custom_call_target="tpu_custom_call" | custom-call | tf_op jit(solution)/shard_map/pallas_call | solution.py:419
  33.7 0.7 %copy.11 = f32[1,4,65,128]{3,1,2,0:T(4,128)} copy(f32[1,4,65,128]{3,1,2,0:T(4,128)S(1)} %bitcast.6) | data formatting | bytes 266240

commit v3 on v2

--- a/solution.py
+++ b/solution.py
@@ -62,14 +62,15 @@
         wb[i, 0, :, 0, i], wb[i, 1, :, 0, i] = cos.T, sin.T
         wb[i, 0, :, 1, i], wb[i, 1, :, 1, i] = -sin.T, cos.T
     wy = np.stack([_right(wy[i].reshape(128, 256)) for i in range(2)])
-    wb = _right(wb.reshape(512, 256))
+    wb = np.concatenate(_halves(wb.reshape(512, 256)), axis=1)
     cos, sin = _trig(np.arange(32), points)
     base = np.zeros((5, 2, 8, GRID))
     base[:4, 0], base[:4, 1] = cos.reshape(4, 8, GRID), -sin.reshape(4, 8, GRID)
     cos, sin = _trig(np.array([RADIUS]), points)
     base[4, 0, 0], base[4, 1, 0] = cos[0] - 1.0, -sin[0]
     base = base.reshape(80, GRID)
-    xf, xb = _left(base.T), _left(base)
+    xf, xb = _left(base.T), np.concatenate(_halves(base), axis=0)
+    xb = np.concatenate([xb, xb], axis=1)
     return zf, wy, xf, xb, wb, zb
 
 
@@ -82,7 +83,7 @@
     return jnp.dot(left, right, preferred_element_type=F32)
 
 
-OFFSETS = [(dx, dz, dc) for dz in (1, 0) for dx in (2, 1, 3, 0) for dc in (1, 0)]
+OFFSETS = [(dx, dz, dc) for dc in (1, 0) for dx in (2, 1, 3, 0) for dz in (1, 0)]
 CHUNKS = [o for o in OFFSETS if o[2] == 0]
 
 
@@ -102,11 +103,10 @@
 
     def plane_peer(offset, sign=1):
         dx, dz, dc = offset
-        return (
-            lax.rem(x_at + sign * dx + 4, 4) * 4
-            + lax.rem(half_at + dz, 2) * 2
-            + lax.rem(core_at + dc, 2)
-        )
+        core_to = lax.rem(core_at + dc, 2)
+        sender = core_at if sign == 1 else core_to
+        x_to = lax.rem(x_at + sign * dx * (1 - 2 * sender) + 4, 4)
+        return x_to * 4 + lax.rem(half_at + dz + sender, 2) * 2 + core_to
 
     side = lax.rem(z_me, 2)
     partner = [
@@ -181,12 +181,6 @@
     own_copy = pltpu.make_async_copy(
         p_h.at[pl.ds(side * 4, 4)], slab.at[y_me, z_me], own_sem
     )
-
-    pl.semaphore_wait(barrier, 33 + n_y - 1)
-    for k in range(1, n_z):
-        gz_copy(k).start()
-    for k in range(1, n_y):
-        gy_copy(0, k).start()
 
     loads[0].wait()
     loads[1].wait()
@@ -205,8 +199,15 @@
         zs[half_of[h]] = mm(
             zf[pl.ds(pl.multiple_of(half_of[h] * 128, 128), 128), :], stacked
         ).reshape(16, 8, 256)
-        for n in range(16):
-            a_copy(h, n).start()
+
+    pl.semaphore_wait(barrier, 33 + n_y - 1)
+    for k in range(1, n_z):
+        gz_copy(k).start()
+    for k in range(1, n_y):
+        gy_copy(0, k).start()
+
+    for n in range(16):
+        a_copy(0, n).start()
     for load in loads[3:]:
         load.start()
     own_copy.start()
@@ -225,6 +226,9 @@
         gz_copy(back).wait_recv()
         for k in range(1, n_y):
             gy_copy(back, k).start()
+
+    for n in range(16):
+        a_copy(1, n).start()
 
     at_zero = lax.broadcasted_iota(jnp.int32, (64, 128), 1) == 31
 
@@ -242,10 +246,11 @@
     def keep(h, value, at):
         high, low = halves(value)
         for orb in range(2):
-            lanes = slice(orb * 128, orb * 128 + 128)
-            bs[h, :, at : at + 16, lanes] = high[orb]
-            bs[h, :, 80 + at : 96 + at, lanes] = high[orb]
-            bs[h, :, 160 + at : 176 + at, lanes] = low[orb]
+            for z in range(4):
+                lanes = slice(z * 256 + orb * 128, z * 256 + orb * 128 + 128)
+                bs[h, at : at + 16, lanes] = high[orb, z]
+                bs[h, 80 + at : 96 + at, lanes] = high[orb, z]
+                bs[h, 160 + at : 176 + at, lanes] = low[orb, z]
 
     def to_columns(h):
         for n in reversed(range(16)):
@@ -272,14 +277,15 @@
 
         if h == 0:
             loads[3].wait()
-        for hx in range(2):
-            high, low = halves(grid[hx])
-            left = jnp.concatenate([high, high, low], axis=1)
-            for i in range(2):
-                turned = mm(left, wy[i]).reshape(2, 4, 2, 8, 256)
-                real = turned[:, :, 0, :, :128] - turned[:, :, 1, :, 128:]
-                imag = turned[:, :, 0, :, 128:] + turned[:, :, 1, :, :128]
-                keep(h, jnp.concatenate([real, imag], axis=2), (2 * hx + i) * 16)
+        high, low = halves(jnp.concatenate(grid, axis=0))
+        left = jnp.concatenate([high, high, low], axis=1)
+        for i in range(2):
+            turned = mm(left, wy[i]).reshape(2, 2, 4, 2, 8, 256)
+            real = turned[:, :, :, 0, :, :128] - turned[:, :, :, 1, :, 128:]
+            imag = turned[:, :, :, 0, :, 128:] + turned[:, :, :, 1, :, :128]
+            both = jnp.concatenate([real, imag], axis=3)
+            for hx in range(2):
+                keep(h, both[hx], (2 * hx + i) * 16)
         keep(h, jnp.broadcast_to(grid[0][:, 31:32], (128, 128)).reshape(2, 4, 16, 128), 64)
 
     def through_planes(h):
@@ -291,15 +297,19 @@
             loads[4].wait()
             loads[5].wait()
 
+        field = mm(xf[...], bs[h])
+        planes = []
         for z in range(4):
-            field = mm(xf[...], bs[h, z])
             plane = jnp.concatenate(
                 [slab[b % n_y, b // n_y, z] for b in range(n_z * n_y)], axis=0
             )
-            high, low = halves(field * jnp.concatenate([plane, plane], axis=1))
-            back = mm(xb[...], jnp.concatenate([high, high, low], axis=0))
+            planes += [plane, plane]
+        high, low = halves(field * jnp.concatenate(planes, axis=1))
+        back = mm(xb[...], jnp.concatenate([high, low], axis=0))
+        back = back[:80] + back[80:]
+        for z in range(4):
             for orb in range(2):
-                lanes = slice(orb * 128, orb * 128 + 128)
+                lanes = slice(z * 256 + orb * 128, z * 256 + orb * 128 + 128)
                 rows = slice(orb * 32 + z * 8, orb * 32 + z * 8 + 8)
                 for xl in range(4):
                     for c in range(2):
@@ -312,9 +322,11 @@
 
         if h == 0:
             loads[6].wait()
+        high, low = halves(cs[h].reshape(128, 512))
+        wide = mm(jnp.concatenate([high, low], axis=0), wb[...])
+        sums = wide[:128, :256] + wide[:128, 256:] + wide[128:, :256]
         for hx in range(2):
-            high, low = halves(cs[h, hx])
-            turned = mm(jnp.concatenate([high, high, low], axis=1), wb[...])
+            turned = sums[hx * 64 : hx * 64 + 64]
             for c in range(2):
                 part = turned[:, c * 128 : c * 128 + 128]
                 if hx == 0:
@@ -338,12 +350,13 @@
             ],
             axis=1,
         )
-        high, low = halves(picked)
+        picked = jnp.concatenate(halves(picked), axis=0)
         for chunk_offset in CHUNKS:
             chunk = plane_peer(chunk_offset) // 2
             lanes = pl.ds(pl.multiple_of(chunk * 256, 256), 256)
             ones = lt[:, lanes]
-            wide = (mm(high, ones) + mm(low, ones)).reshape(8, 16, 256)
+            wide = mm(picked, ones)
+            wide = (wide[:128] + wide[128:]).reshape(8, 16, 256)
             d_here = jnp.broadcast_to(sm_ref[0:1, lanes] & 7, (16, 256))
             total = wide[0]
             for d in range(1, 8):
@@ -358,8 +371,8 @@
                     b_copy(h, n).start()
 
     to_columns(0)
+    through_planes(0)
     to_columns(1)
-    through_planes(0)
     through_planes(1)
 
     for k in range(1, n_z):
@@ -408,7 +421,7 @@
         pltpu.VMEM((4, 16, 2048), BF),
         pltpu.VMEM((2, 256, 2048), BF),
         pltpu.VMEM((2, 2, 128, 128), F32),
-        pltpu.VMEM((2, 4, 240, 256), BF),
+        pltpu.VMEM((2, 240, 1024), BF),
         pltpu.VMEM((2, 2, 64, 512), F32),
         pltpu.VMEM((2, 2, 64, 128), F32),
         pltpu.VMEM((2, 2, 128, 128), F32),

time: 34.4 us -> 32.8 us (0.953)
  Pallas kernels: 33.7 us -> 32 us
    pallas_call x1, Pallas kernels: 33.7 us -> 32 us  [per_device(): pl.pallas_call(functools.partial(kernel, n_z, n_y), out_shape=jax.ShapeDt...]
where the time goes in v3:
time: 32.8 us; the launch traced here: 32.7 us
  Pallas kernels  32 us (98%)
  local copies, waits for them, and re-layouts  0.66 us (2%)
    pallas_call x1, Pallas kernels, per_device(): pl.pallas_call(functools.partial(kernel, n_z, n_y), out_shape=jax.ShapeDt...  32 us
    unnamed x1, local copies, waits for them, and re-layouts  0.66 us

profile of v3, /device:TPU:1, one launch (start us, length us, event | category | flops | bytes accessed | tf_op | source)
XLA Modules:
  0.0 32.7 jit_solution(5115736268132293122)
XLA Ops:
  0.0 32.0 %shard_map.91 = f32[65,4,128]{2,1,0:T(4,128)S(1)} custom-call(f32[65,4,128]{2,1,0:T(4,128)} %bitcast.7, f32[8,8,128]{2,1,0:T(8,128)} %p_h.1, s32[3,2048]{1,0:T(4,128)} %sm_h.1, bf16[256,480]{1,0:T(8,128)(2,1)} %constant.12.clone.zf_h, bf16[2,384,256]{2,1,0:T(8,128)(2,1)} %constant.13.clone.wy_h, bf16[128,240]{1,0:T(8,128)(2,1)} %constant.14.clone.xf_h, ...), custom_call_target="tpu_custom_call" | custom-call | tf_op jit(solution)/shard_map/pallas_call | solution.py:432
  32.0 0.7 %copy.11 = f32[1,4,65,128]{3,1,2,0:T(4,128)} copy(f32[1,4,65,128]{3,1,2,0:T(4,128)S(1)} %bitcast.6) | data formatting | bytes 266240

commit v4 on v3

--- a/solution.py
+++ b/solution.py
@@ -201,9 +201,9 @@
         ).reshape(16, 8, 256)
 
     pl.semaphore_wait(barrier, 33 + n_y - 1)
-    for k in range(1, n_z):
+    for k in (2, 1, 3):
         gz_copy(k).start()
-    for k in range(1, n_y):
+    for k in (2, 1, 3):
         gy_copy(0, k).start()
 
     for n in range(16):
@@ -224,7 +224,7 @@
 
     for back in sorted(range(1, n_z), key=lambda k: min(k, n_z - k)):
         gz_copy(back).wait_recv()
-        for k in range(1, n_y):
+        for k in (2, 1, 3):
             gy_copy(back, k).start()
 
     for n in range(16):

time: 32.8 us -> 32.6 us (level)
  no operation moved by 1% of the time
where the time goes in v4:
time: 32.6 us; the launch traced here: 32.5 us
  Pallas kernels  31.8 us (98%)
  local copies, waits for them, and re-layouts  0.66 us (2%)
    pallas_call x1, Pallas kernels, per_device(): pl.pallas_call(functools.partial(kernel, n_z, n_y), out_shape=jax.ShapeDt...  31.8 us
    unnamed x1, local copies, waits for them, and re-layouts  0.66 us

profile of v4, /device:TPU:1, one launch (start us, length us, event | category | flops | bytes accessed | tf_op | source)
XLA Modules:
  0.0 32.5 jit_solution(12978404942701704773)
XLA Ops:
  0.0 31.8 %shard_map.91 = f32[65,4,128]{2,1,0:T(4,128)S(1)} custom-call(f32[65,4,128]{2,1,0:T(4,128)} %bitcast.7, f32[8,8,128]{2,1,0:T(8,128)} %p_h.1, s32[3,2048]{1,0:T(4,128)} %sm_h.1, bf16[256,480]{1,0:T(8,128)(2,1)} %constant.12.clone.zf_h, bf16[2,384,256]{2,1,0:T(8,128)(2,1)} %constant.13.clone.wy_h, bf16[128,240]{1,0:T(8,128)(2,1)} %constant.14.clone.xf_h, ...), custom_call_target="tpu_custom_call" | custom-call | tf_op jit(solution)/shard_map/pallas_call | solution.py:432
  31.8 0.7 %copy.11 = f32[1,4,65,128]{3,1,2,0:T(4,128)} copy(f32[1,4,65,128]{3,1,2,0:T(4,128)S(1)} %bitcast.6) | data formatting | bytes 266240

commit v5 on v4

--- a/solution.py
+++ b/solution.py
@@ -83,7 +83,7 @@
     return jnp.dot(left, right, preferred_element_type=F32)
 
 
-OFFSETS = [(dx, dz, dc) for dc in (1, 0) for dx in (2, 1, 3, 0) for dz in (1, 0)]
+OFFSETS = [(dx, dz, dc) for dx in (2, 1, 3, 0) for dz in (1, 0) for dc in (1, 0)]
 CHUNKS = [o for o in OFFSETS if o[2] == 0]
 
 

time: 32.6 us -> 32.6 us (level)
  no operation moved by 1% of the time
where the time goes in v5:
time: 32.6 us
  Pallas kernels  31.9 us (98%)
  local copies, waits for them, and re-layouts  0.66 us (2%)
    pallas_call x1, Pallas kernels, per_device(): pl.pallas_call(functools.partial(kernel, n_z, n_y), out_shape=jax.ShapeDt...  31.9 us
    unnamed x1, local copies, waits for them, and re-layouts  0.66 us

profile of v5, /device:TPU:1, one launch (start us, length us, event | category | flops | bytes accessed | tf_op | source)
XLA Modules:
  0.0 32.6 jit_solution(1751238536484485541)
XLA Ops:
  0.0 31.9 %shard_map.91 = f32[65,4,128]{2,1,0:T(4,128)S(1)} custom-call(f32[65,4,128]{2,1,0:T(4,128)} %bitcast.7, f32[8,8,128]{2,1,0:T(8,128)} %p_h.1, s32[3,2048]{1,0:T(4,128)} %sm_h.1, bf16[256,480]{1,0:T(8,128)(2,1)} %constant.12.clone.zf_h, bf16[2,384,256]{2,1,0:T(8,128)(2,1)} %constant.13.clone.wy_h, bf16[128,240]{1,0:T(8,128)(2,1)} %constant.14.clone.xf_h, ...), custom_call_target="tpu_custom_call" | custom-call | tf_op jit(solution)/shard_map/pallas_call | solution.py:432
  31.9 0.7 %copy.11 = f32[1,4,65,128]{3,1,2,0:T(4,128)} copy(f32[1,4,65,128]{3,1,2,0:T(4,128)S(1)} %bitcast.6) | data formatting | bytes 266240
